TPU v7x, 256 devices: a whole 4x4x8 slice. The times are simulated.
256 devices in a mesh: sub: 64 (over y, z, core), rhs: 4 (over x).
Axes of the slice: x: 4, y: 4, z: 8, core: 2. Of those that a mesh axis runs over, the one named last changes fastest.
Arguments:
- right_side: float32 [256, 252, 512], P('sub', None, 'rhs'), parts along dimension 2, may hold values from -70 to 70
- coupling: bfloat16 [256, 508032], P('sub'), may hold values from -0.0625 to 0.0625
- neighbours: int32 [256, 8], P('sub'), may hold values from 0 to 255, as said below
- inverse: bfloat16 [64, 1512, 1512], P('sub'), may hold values from -1 to 1
- margin: int32 [64, 2], P('sub'), may hold values from 0 to 255, as said below
- counts: int32 [64], P('sub'), may hold values from 1 to 4, as said below
Outputs:
- solution: float32 [256, 252, 512], P('sub', None, 'rhs'), parts along dimension 2
There are 4 independent parts, one for each index of `rhs`. A program takes and returns all parts, laid end to end along the dimension named above; an argument that names none is the same for every part. Nothing has to cross between parts.
Inputs may be any that keep to these rules, and one draw needn't show every extreme that they name: `counts`: every subdomain holds 1 to 4 live spheres, and some subdomain holds exactly 4. `neighbours`: every entry of row i is a live sphere slot of the subdomain of i or of a subdomain adjacent to it (index one lower or one higher). `margin`: for subdomain d the first 1 entries are live slots of subdomain d - 1 (of subdomain 0 itself for d = 0), the last 1 live slots of subdomain d + 1 (of the last subdomain itself for the last one).
All inputs are finite; a program needn't handle non-finite values.
Results may differ from a plain program's by a relative error of at most 0.0055.
Values may be sent and summed in bfloat16 or wider, within the bound.
No kernel may reach another device: no remote copies, remote signals or barrier semaphores. Data moves between devices by JAX's collectives and lax.ppermute only.
A program may use at most 64 MiB of HBM per device.

v0:
```python
import jax
import jax.numpy as jnp
from jax import lax
from jax.sharding import PartitionSpec as P

epsilon = 1e-06


def extended_2(block, sides, width):
    for axis, dim in sides:
        count = lax.axis_size(axis)
        forward = [(i, i + 1) for i in range(count - 1)]
        backward = [(target, source) for source, target in forward]
        low = lax.ppermute(
            lax.slice_in_dim(block, block.shape[dim] - width, None, axis=dim), axis, forward
        )
        high = lax.ppermute(lax.slice_in_dim(block, 0, width, axis=dim), axis, backward)
        block = jnp.concatenate([low, block, high], axis=dim)
    return block


def passed_along(x, axis, by):
    size = lax.axis_size(axis)
    pairs = [(i, i + by) for i in range(size) if 0 <= i + by < size]
    return lax.ppermute(x, axis, pairs)


def inner(left, right):
    return jnp.sum(left * right, axis=(0, 1))


def global_norm(vector):
    return jnp.sqrt(lax.psum(inner(vector, vector), "sub") + epsilon)


def body(right_side, coupling, neighbours, inverse, margin, counts):
    rows = right_side.shape[0]
    width = right_side.shape[1]
    fields = right_side.shape[2]
    blocks = neighbours.shape[1]
    matrices = coupling.reshape(rows, blocks, width, width)
    here = lax.axis_index("sub")
    slots = jnp.arange(rows, dtype=jnp.int32)
    alive = (slots < counts[0]).astype(jnp.float32)[:, None, None]
    offset = (here - 1) * rows
    frame_slots = jnp.arange(3 * rows, dtype=jnp.int32)
    extra_slots = margin[0]
    picker = (extra_slots[:, None] - offset == frame_slots[None, :]).astype(jnp.float32)
    picker_low = picker.astype(jnp.bfloat16)
    near_local = (neighbours - offset).reshape(-1)

    def precondition(vector):
        rounded = vector.astype(jnp.bfloat16)
        frame = extended_2(rounded, (("sub", 0),), rows)
        extra = jnp.einsum(
            "hq,qwr->hwr", picker_low, frame, preferred_element_type=jnp.float32
        ).astype(jnp.bfloat16)
        extended = jnp.concatenate([rounded, extra], axis=0).reshape(-1, fields)
        output = jnp.dot(inverse[0], extended, preferred_element_type=jnp.float32)
        output = output.reshape(-1, width, fields)
        spill = output[rows:]
        framed = jnp.einsum("hq,hwr->qwr", picker, spill, precision=lax.Precision.HIGHEST)
        from_right = passed_along(framed[:rows].astype(jnp.bfloat16), "sub", -1).astype(jnp.float32)
        from_left = passed_along(framed[2 * rows :].astype(jnp.bfloat16), "sub", 1).astype(
            jnp.float32
        )
        result = output[:rows] + framed[rows : 2 * rows] + from_right + from_left
        return result * alive

    def apply_system(vector):
        rounded = vector.astype(jnp.bfloat16)
        frame = extended_2(rounded, (("sub", 0),), rows)
        nearby = jnp.take(frame, near_local, axis=0).reshape(rows, blocks, width, fields)
        product = jnp.einsum("pkvw,pkwr->pvr", matrices, nearby, preferred_element_type=jnp.float32)
        return (vector + product) * alive

    start = right_side * alive
    initial = global_norm(start)
    basis_one = start / initial[None, None, :]
    pre_one = precondition(basis_one)
    image = apply_system(pre_one)
    h_one_one = lax.psum(inner(basis_one, image), "sub")
    image = image - h_one_one[None, None, :] * basis_one
    h_two_one = global_norm(image)
    basis_two = image / h_two_one[None, None, :]
    pre_two = precondition(basis_two)
    image = apply_system(pre_two)
    h_one_two = lax.psum(inner(basis_one, image), "sub")
    image = image - h_one_two[None, None, :] * basis_one
    h_two_two = lax.psum(inner(basis_two, image), "sub")
    image = image - h_two_two[None, None, :] * basis_two
    h_three_two = global_norm(image)
    gram_aa = h_one_one * h_one_one + h_two_one * h_two_one
    gram_ab = h_one_one * h_one_two + h_two_one * h_two_two
    gram_bb = h_one_two * h_one_two + h_two_two * h_two_two + h_three_two * h_three_two
    determinant = gram_aa * gram_bb - gram_ab * gram_ab
    weight_one = initial * (gram_bb * h_one_one - gram_ab * h_one_two) / determinant
    weight_two = initial * (gram_aa * h_one_two - gram_ab * h_one_one) / determinant
    return weight_one[None, None, :] * pre_one + weight_two[None, None, :] * pre_two


def solution(mesh):
    placed = (
        P("sub", None, "rhs"),
        P("sub", None),
        P("sub", None),
        P("sub", None, None),
        P("sub", None),
        P("sub"),
    )
    return jax.shard_map(
        body, mesh=mesh, in_specs=placed, out_specs=P("sub", None, "rhs"), check_vma=False
    )
```

profile of v0, /device:TPU:1, one launch (start us, length us, event | category | flops | bytes accessed | tf_op | source)
XLA Modules:
  0.0 864.6 jit_solution(13683966303049429386)
XLA Ops:
  2.1 128.3 %psum.42 = f32[128]{0:T(128)S(1)} all-reduce(f32[128]{0:T(128)S(1)} %multiply_reduce_fusion.5), channel_id=1, replica_groups=mesh['sub'=64,'rhs'=4] {'sub'}, use_global_device_ids=true, to_apply=%region_1.0 | all-reduce | flops 128 | bytes 1024 | tf_op jit(solution)/shard_map/psum | solution.py:33
  131.6 6.9 collective-permute-start.1
  141.1 2.6 collective-permute-done
  144.7 3.7 fusion.4
  149.2 2.2 fusion.51
  154.2 4.4 collective-permute-start.3
  162.2 2.4 fusion.46
  166.5 4.6 collective-permute-start.4
  171.1 6.9 reshape.82
  178.0 13.2 %reshape.53 = bf16[4,8,252,252]{3,2,1,0:T(8,128)(2,1)} reshape(bf16[2032128]{0:T(1024)(128)(2,1)} %reshape.82) | data formatting | bytes 8128512 | tf_op jit(solution)/shard_map/reshape | solution.py:41
  196.9 121.4 %psum.43 = f32[128]{0:T(128)S(1)} all-reduce(f32[128]{0:T(128)S(1)} %get-tuple-element.12), channel_id=1, replica_groups=mesh['sub'=64,'rhs'=4] {'sub'}, use_global_device_ids=true, to_apply=%region_3.5 | all-reduce | flops 128 | bytes 1024 | tf_op jit(solution)/shard_map/psum | solution.py:82
  318.6 126.5 %psum.44 = f32[128]{0:T(128)S(1)} all-reduce(f32[128]{0:T(128)S(1)} %multiply_reduce_fusion.3), channel_id=1, replica_groups=mesh['sub'=64,'rhs'=4] {'sub'}, use_global_device_ids=true, to_apply=%region_5.7 | all-reduce | flops 128 | bytes 1024 | tf_op jit(solution)/shard_map/psum | solution.py:33
  446.1 2.5 collective-permute-start.7
  448.6 3.0 collective-permute-start.6
  451.7 2.1 collective-permute-done.7
  455.9 3.7 fusion.7
  460.4 2.2 fusion.52
  465.4 4.4 collective-permute-start.9
  473.4 2.5 fusion.42
  477.7 4.4 collective-permute-start.10
  482.1 2.1 collective-permute-done.11
  491.1 120.7 %psum.45 = f32[128]{0:T(128)S(1)} all-reduce(f32[128]{0:T(128)S(1)} %get-tuple-element.6), channel_id=1, replica_groups=mesh['sub'=64,'rhs'=4] {'sub'}, use_global_device_ids=true, to_apply=%region_7.9 | all-reduce | flops 128 | bytes 1024 | tf_op jit(solution)/shard_map/psum | solution.py:88
  612.1 127.2 %psum.46 = f32[128]{0:T(128)S(1)} all-reduce(f32[128]{0:T(128)S(1)} %multiply_reduce_fusion.1), channel_id=1, replica_groups=mesh['sub'=64,'rhs'=4] {'sub'}, use_global_device_ids=true, to_apply=%region_9.11 | all-reduce | flops 128 | bytes 1024 | tf_op jit(solution)/shard_map/psum | solution.py:90
  739.6 124.0 %psum.47 = f32[128]{0:T(128)S(1)} all-reduce(f32[128]{0:T(128)S(1)} %multiply_reduce_fusion), channel_id=1, replica_groups=mesh['sub'=64,'rhs'=4] {'sub'}, use_global_device_ids=true, to_apply=%region_11.13 | all-reduce | flops 128 | bytes 1024 | tf_op jit(solution)/shard_map/psum | solution.py:33
  (75 shorter events, 41.7 us)
Async XLA Ops:
  131.6 9.5 %collective-permute-start.1 = (bf16[4,252,128]{2,0,1:T(4,128)(2,1)S(1)}, bf16[4,252,128]{2,0,1:T(4,128)(2,1)S(1)}, u32[]{:S(2)}, u32[]{:S(2)}) collective-permute-start(bf16[4,252,128]{2,0,1:T(4,128)(2,1)S(1)} %get-tuple-element.16), channel_id=1, source_target_pairs={{4,0},{8,4},{12,8},{16,12},{20,16},{24,20},{28,24},{32,28},{36,32}... | collective-permute-start | bytes 774152 | tf_op jit(solution)/shard_map/ppermute | solution.py:17
  138.5 5.2 collective-permute-start
  149.2 9.4 %copy-start.6 = (s32[4,8]{1,0:T(4,128)S(1)}, s32[4,8]{1,0:T(4,128)}, u32[]{:S(2)}) copy-start(s32[4,8]{1,0:T(4,128)} %param.10) | copy-start | bytes 388
  152.3 8.7 %collective-permute-start.2 = (bf16[4,252,128]{2,0,1:T(4,128)(2,1)}, bf16[4,252,128]{2,0,1:T(4,128)(2,1)}, u32[]{:S(2)}, u32[]{:S(2)}) collective-permute-start(bf16[4,252,128]{2,0,1:T(4,128)(2,1)} %get-tuple-element.20), channel_id=1, source_target_pairs={{4,0},{8,4},{12,8},{16,12},{20,16},{24,20},{28,24},{32,28},{36,32}... | collective-permute-start | bytes 774152 | tf_op jit(solution)/shard_map/ppermute | solution.py:25
  154.2 8.0 collective-permute-start.3
  164.6 26.6 %collective-permute-start.5 = (bf16[4,252,128]{2,0,1:T(4,128)(2,1)S(1)}, bf16[4,252,128]{2,0,1:T(4,128)(2,1)S(1)}, u32[]{:S(2)}, u32[]{:S(2)}) collective-permute-start(bf16[4,252,128]{2,0,1:T(4,128)(2,1)S(1)} %get-tuple-element.14), channel_id=1, source_target_pairs={{4,0},{8,4},{12,8},{16,12},{20,16},{24,20},{28,24},{32,28},{36,32}... | collective-permute-start | bytes 774152 | tf_op jit(solution)/shard_map/ppermute | solution.py:17
  166.5 24.7 %collective-permute-start.4 = (bf16[4,252,128]{2,0,1:T(4,128)(2,1)S(1)}, bf16[4,252,128]{2,0,1:T(4,128)(2,1)S(1)}, u32[]{:S(2)}, u32[]{:S(2)}) collective-permute-start(bf16[4,252,128]{2,0,1:T(4,128)(2,1)S(1)} %get-tuple-element.14), channel_id=1, source_target_pairs={{0,4},{4,8},{8,12},{12,16},{16,20},{20,24},{24,28},{28,32},{32,36}... | collective-permute-start | bytes 774152 | tf_op jit(solution)/shard_map/ppermute | solution.py:14
  192.9 2.2 copy-start
  195.1 1.3 copy-start.2
  446.1 7.6 collective-permute-start.7
  448.6 6.3 collective-permute-start.6
  463.5 8.7 %collective-permute-start.8 = (bf16[4,252,128]{2,0,1:T(4,128)(2,1)}, bf16[4,252,128]{2,0,1:T(4,128)(2,1)}, u32[]{:S(2)}, u32[]{:S(2)}) collective-permute-start(bf16[4,252,128]{2,0,1:T(4,128)(2,1)} %get-tuple-element.18), channel_id=1, source_target_pairs={{4,0},{8,4},{12,8},{16,12},{20,16},{24,20},{28,24},{32,28},{36,32}... | collective-permute-start | bytes 774152 | tf_op jit(solution)/shard_map/ppermute | solution.py:25
  465.4 8.0 collective-permute-start.9
  475.8 8.4 collective-permute-start.11
  477.7 7.6 collective-permute-start.10
  487.1 2.2 copy-start.1
  489.3 1.3 copy-start.4
  490.5 121.2 %copy-start.5 = (f32[4,252,128]{2,0,1:T(4,128)S(1)}, f32[4,252,128]{2,0,1:T(4,128)}, u32[]{:S(2)}) copy-start(f32[4,252,128]{2,0,1:T(4,128)} %get-tuple-element.11) | copy-start | bytes 1548292
  490.5 373.1 %copy-start.3 = (f32[4,252,128]{2,0,1:T(4,128)S(1)}, f32[4,252,128]{2,0,1:T(4,128)}, u32[]{:S(2)}) copy-start(f32[4,252,128]{2,0,1:T(4,128)} %get-tuple-element.15) | copy-start | bytes 1548292
where the time goes:
time: 866 us; the launch traced here: 865 us
  blocking collectives  748 us (86%)
  starting transfers between devices  39.8 us (5%)
  local copies, waits for them, and re-layouts  33.8 us (4%)
  matrix products  15.4 us (2%)
  other arithmetic  14.1 us (2%)
  waiting for transfers between devices  12.3 us (1%)
    psum x3, blocking collectives, global_norm(): return jnp.sqrt(lax.psum(inner(vector, vector), 'sub') + epsilon)  379 us
    psum x1, blocking collectives, body(): h_two_two = lax.psum(inner(basis_two, image), 'sub')  127 us
    psum x1, blocking collectives, body(): h_one_one = lax.psum(inner(basis_one, image), 'sub')  121 us
    psum x1, blocking collectives, body(): h_one_two = lax.psum(inner(basis_one, image), 'sub')  121 us
  transfers between devices with their start and end apart: 12, of which 9 were waited for; matrix products, arithmetic and copies ran while one was open for 3% of the time, Pallas kernels for 0%

commit v1 on v0

--- a/solution.py
+++ b/solution.py
@@ -79,7 +79,12 @@
     basis_one = start / initial[None, None, :]
     pre_one = precondition(basis_one)
     image = apply_system(pre_one)
-    h_one_one = lax.psum(inner(basis_one, image), "sub")
+
+    def test_quotas(panel, bus_axis):
+        value_now = jnp.sum(lax.all_gather(panel, bus_axis), axis=0)
+        return value_now
+
+    h_one_one = test_quotas(inner(basis_one, image), "sub")
     image = image - h_one_one[None, None, :] * basis_one
     h_two_one = global_norm(image)
     basis_two = image / h_two_one[None, None, :]

time: 866 us -> 779 us (0.90)
  blocking collectives: 748 us -> 660 us
    psum x1 -> x0, blocking collectives: 121 us -> none  [body(): h_one_one = lax.psum(inner(basis_one, image), 'sub')]
    all_gather x0 -> x1, blocking collectives: none -> 36.1 us  [test_quotas(): value_now = jnp.sum(lax.all_gather(panel, bus_axis), axis=0)]
where the time goes in v1:
time: 779 us; the launch traced here: 778 us
  blocking collectives  660 us (85%)
  starting transfers between devices  41.2 us (5%)
  local copies, waits for them, and re-layouts  33.8 us (4%)
  matrix products  15.4 us (2%)
  other arithmetic  14.2 us (2%)
  waiting for transfers between devices  12 us (2%)
    psum x3, blocking collectives, global_norm(): return jnp.sqrt(lax.psum(inner(vector, vector), 'sub') + epsilon)  376 us
    psum x1, blocking collectives, body(): h_two_two = lax.psum(inner(basis_two, image), 'sub')  127 us
    psum x1, blocking collectives, body(): h_one_two = lax.psum(inner(basis_one, image), 'sub')  121 us
    all_gather x1, blocking collectives, test_quotas(): value_now = jnp.sum(lax.all_gather(panel, bus_axis), axis=0)  36.1 us
  transfers between devices with their start and end apart: 12, of which 9 were waited for; matrix products, arithmetic and copies ran while one was open for 3% of the time, Pallas kernels for 0%

profile of v1, /device:TPU:1, one launch (start us, length us, event | category | flops | bytes accessed | tf_op | source)
XLA Modules:
  0.0 777.6 jit_solution(6537542247033549400)
XLA Ops:
  2.1 128.3 %psum.35 = f32[128]{0:T(128)S(1)} all-reduce(f32[128]{0:T(128)S(1)} %multiply_reduce_fusion.5), channel_id=1, replica_groups=mesh['sub'=64,'rhs'=4] {'sub'}, use_global_device_ids=true, to_apply=%region_1.0 | all-reduce | flops 128 | bytes 1024 | tf_op jit(solution)/shard_map/psum | solution.py:33
  131.6 6.9 collective-permute-start.1
  138.5 1.9 collective-permute-start
  141.1 2.6 collective-permute-done
  144.7 3.7 fusion.4
  149.2 2.2 fusion.51
  154.2 4.4 collective-permute-start.3
  162.2 2.4 fusion.46
  166.5 4.6 collective-permute-start.4
  171.1 6.9 reshape.86
  178.0 13.2 %reshape.53 = bf16[4,8,252,252]{3,2,1,0:T(8,128)(2,1)} reshape(bf16[2032128]{0:T(1024)(128)(2,1)} %reshape.86) | data formatting | bytes 8128512 | tf_op jit(solution)/shard_map/reshape | solution.py:41
  196.9 36.1 %all-gather.1 = f32[64,1,128]{2,1,0:T(1,128)S(1)} all-gather(f32[1,1,128]{2,1,0:T(1,128)S(1)} %bitcast.55), channel_id=2, replica_groups=mesh['sub'=64,'rhs'=4] {'sub'}, dimensions={0}, use_global_device_ids=true | all-gather | bytes 33280 | tf_op jit(solution)/shard_map/all_gather | solution.py:84
  233.3 123.6 %psum.36 = f32[128]{0:T(128)S(1)} all-reduce(f32[128]{0:T(128)S(1)} %multiply_reduce_fusion.3), channel_id=1, replica_groups=mesh['sub'=64,'rhs'=4] {'sub'}, use_global_device_ids=true, to_apply=%region_5.7 | all-reduce | flops 128 | bytes 1024 | tf_op jit(solution)/shard_map/psum | solution.py:33
  357.9 4.8 collective-permute-start.7
  362.7 1.9 collective-permute-start.6
  365.5 2.4 collective-permute-done.6
  368.9 3.7 fusion.7
  373.4 2.2 fusion.52
  378.4 4.4 collective-permute-start.9
  386.3 2.5 fusion.42
  390.7 4.6 collective-permute-start.10
  404.0 120.7 %psum.37 = f32[128]{0:T(128)S(1)} all-reduce(f32[128]{0:T(128)S(1)} %get-tuple-element.6), channel_id=1, replica_groups=mesh['sub'=64,'rhs'=4] {'sub'}, use_global_device_ids=true, to_apply=%region_7.9 | all-reduce | flops 128 | bytes 1024 | tf_op jit(solution)/shard_map/psum | solution.py:93
  525.0 127.2 %psum.38 = f32[128]{0:T(128)S(1)} all-reduce(f32[128]{0:T(128)S(1)} %multiply_reduce_fusion.1), channel_id=1, replica_groups=mesh['sub'=64,'rhs'=4] {'sub'}, use_global_device_ids=true, to_apply=%region_9.11 | all-reduce | flops 128 | bytes 1024 | tf_op jit(solution)/shard_map/psum | solution.py:95
  652.6 124.0 %psum.39 = f32[128]{0:T(128)S(1)} all-reduce(f32[128]{0:T(128)S(1)} %multiply_reduce_fusion), channel_id=1, replica_groups=mesh['sub'=64,'rhs'=4] {'sub'}, use_global_device_ids=true, to_apply=%region_11.13 | all-reduce | flops 128 | bytes 1024 | tf_op jit(solution)/shard_map/psum | solution.py:33
  (76 shorter events, 41.4 us)
Async XLA Ops:
  131.6 9.5 %collective-permute-start.1 = (bf16[4,252,128]{2,0,1:T(4,128)(2,1)S(1)}, bf16[4,252,128]{2,0,1:T(4,128)(2,1)S(1)}, u32[]{:S(2)}, u32[]{:S(2)}) collective-permute-start(bf16[4,252,128]{2,0,1:T(4,128)(2,1)S(1)} %get-tuple-element.16), channel_id=1, source_target_pairs={{4,0},{8,4},{12,8},{16,12},{20,16},{24,20},{28,24},{32,28},{36,32}... | collective-permute-start | bytes 774152 | tf_op jit(solution)/shard_map/ppermute | solution.py:17
  138.5 5.2 collective-permute-start
  149.2 9.4 %copy-start.6 = (s32[4,8]{1,0:T(4,128)S(1)}, s32[4,8]{1,0:T(4,128)}, u32[]{:S(2)}) copy-start(s32[4,8]{1,0:T(4,128)} %param.10) | copy-start | bytes 388
  152.3 8.7 %collective-permute-start.2 = (bf16[4,252,128]{2,0,1:T(4,128)(2,1)}, bf16[4,252,128]{2,0,1:T(4,128)(2,1)}, u32[]{:S(2)}, u32[]{:S(2)}) collective-permute-start(bf16[4,252,128]{2,0,1:T(4,128)(2,1)} %get-tuple-element.20), channel_id=1, source_target_pairs={{4,0},{8,4},{12,8},{16,12},{20,16},{24,20},{28,24},{32,28},{36,32}... | collective-permute-start | bytes 774152 | tf_op jit(solution)/shard_map/ppermute | solution.py:25
  154.2 8.0 %collective-permute-start.3 = (bf16[4,252,128]{2,0,1:T(4,128)(2,1)}, bf16[4,252,128]{2,0,1:T(4,128)(2,1)}, u32[]{:S(2)}, u32[]{:S(2)}) collective-permute-start(bf16[4,252,128]{2,0,1:T(4,128)(2,1)} %get-tuple-element.21), channel_id=1, source_target_pairs={{0,4},{4,8},{8,12},{12,16},{16,20},{20,24},{24,28},{28,32},{32,36}... | collective-permute-start | bytes 774152 | tf_op jit(solution)/shard_map/ppermute | solution.py:25
  164.6 26.6 %collective-permute-start.5 = (bf16[4,252,128]{2,0,1:T(4,128)(2,1)S(1)}, bf16[4,252,128]{2,0,1:T(4,128)(2,1)S(1)}, u32[]{:S(2)}, u32[]{:S(2)}) collective-permute-start(bf16[4,252,128]{2,0,1:T(4,128)(2,1)S(1)} %get-tuple-element.14), channel_id=1, source_target_pairs={{4,0},{8,4},{12,8},{16,12},{20,16},{24,20},{28,24},{32,28},{36,32}... | collective-permute-start | bytes 774152 | tf_op jit(solution)/shard_map/ppermute | solution.py:17
  166.5 24.7 %collective-permute-start.4 = (bf16[4,252,128]{2,0,1:T(4,128)(2,1)S(1)}, bf16[4,252,128]{2,0,1:T(4,128)(2,1)S(1)}, u32[]{:S(2)}, u32[]{:S(2)}) collective-permute-start(bf16[4,252,128]{2,0,1:T(4,128)(2,1)S(1)} %get-tuple-element.14), channel_id=1, source_target_pairs={{0,4},{4,8},{8,12},{12,16},{16,20},{20,24},{24,28},{28,32},{32,36}... | collective-permute-start | bytes 774152 | tf_op jit(solution)/shard_map/ppermute | solution.py:14
  192.9 2.2 copy-start
  195.1 1.3 copy-start.2
  357.9 7.6 collective-permute-start.7
  362.7 5.2 collective-permute-start.6
  376.5 8.7 %collective-permute-start.8 = (bf16[4,252,128]{2,0,1:T(4,128)(2,1)}, bf16[4,252,128]{2,0,1:T(4,128)(2,1)}, u32[]{:S(2)}, u32[]{:S(2)}) collective-permute-start(bf16[4,252,128]{2,0,1:T(4,128)(2,1)} %get-tuple-element.18), channel_id=1, source_target_pairs={{4,0},{8,4},{12,8},{16,12},{20,16},{24,20},{28,24},{32,28},{36,32}... | collective-permute-start | bytes 774152 | tf_op jit(solution)/shard_map/ppermute | solution.py:25
  378.4 8.0 %collective-permute-start.9 = (bf16[4,252,128]{2,0,1:T(4,128)(2,1)}, bf16[4,252,128]{2,0,1:T(4,128)(2,1)}, u32[]{:S(2)}, u32[]{:S(2)}) collective-permute-start(bf16[4,252,128]{2,0,1:T(4,128)(2,1)} %get-tuple-element.19), channel_id=1, source_target_pairs={{0,4},{4,8},{8,12},{12,16},{16,20},{20,24},{24,28},{28,32},{32,36}... | collective-permute-start | bytes 774152 | tf_op jit(solution)/shard_map/ppermute | solution.py:25
  388.8 8.4 %collective-permute-start.11 = (bf16[4,252,128]{2,0,1:T(4,128)(2,1)S(1)}, bf16[4,252,128]{2,0,1:T(4,128)(2,1)S(1)}, u32[]{:S(2)}, u32[]{:S(2)}) collective-permute-start(bf16[4,252,128]{2,0,1:T(4,128)(2,1)S(1)} %get-tuple-element.8), channel_id=1, source_target_pairs={{4,0},{8,4},{12,8},{16,12},{20,16},{24,20},{28,24},{32,28},{36,32}... | collective-permute-start | bytes 774152 | tf_op jit(solution)/shard_map/ppermute | solution.py:17
  390.7 7.6 collective-permute-start.10
  400.1 2.2 copy-start.1
  402.2 1.3 copy-start.4
  403.5 121.2 %copy-start.5 = (f32[4,252,128]{2,0,1:T(4,128)S(1)}, f32[4,252,128]{2,0,1:T(4,128)}, u32[]{:S(2)}) copy-start(f32[4,252,128]{2,0,1:T(4,128)} %get-tuple-element.11) | copy-start | bytes 1548292
  403.5 373.1 %copy-start.3 = (f32[4,252,128]{2,0,1:T(4,128)S(1)}, f32[4,252,128]{2,0,1:T(4,128)}, u32[]{:S(2)}) copy-start(f32[4,252,128]{2,0,1:T(4,128)} %get-tuple-element.15) | copy-start | bytes 1548292
